TPU v7x, 128 devices: a whole 4x4x4 slice. The times are simulated.
128 devices in a mesh: dp: 8 (over z_lo, x), fsdp: 16 (over y, z_hi, core).
Axes of the slice: x: 4, y: 4, z: 4 (z_hi: 2, z_lo: 2; z = z_hi * 2 + z_lo), core: 2. Of those that a mesh axis runs over, the one named last changes fastest.
Arguments:
- queries: bfloat16 [65536, 2048], P(('dp', 'fsdp')), may hold values from -6 to 6
- keys: bfloat16 [65536, 2048], P(('dp', 'fsdp')), may hold values from -6 to 6
- values: bfloat16 [65536, 2048], P(('dp', 'fsdp')), may hold values from -6 to 6
- attn_out: bfloat16 [65536, 2048], P(('dp', 'fsdp')), may hold values from -24 to 24
- out_grad: bfloat16 [65536, 2048], P(('dp', 'fsdp')), may hold values from -6 to 6
- log_norm: float32 [65536, 16], P(('dp', 'fsdp')), may hold values from 4 to 7
- segment_ids: int32 [128, 4], P(('dp', 'fsdp')), may hold values from 0 to 3, as said below
- kept_tokens: int32 [128, 4], P(('dp', 'fsdp')), may hold values from 0 to 512, as said below
- out_weight: bfloat16 [2048, 2048], P('fsdp'), may hold values from -0.125 to 0.125
Outputs:
- query_grad: bfloat16 [65536, 2048], P(('dp', 'fsdp'))
- key_grad: bfloat16 [65536, 2048], P(('dp', 'fsdp'))
- value_grad: bfloat16 [65536, 2048], P(('dp', 'fsdp'))
- weight_grad: float32 [2048, 2048], P('fsdp')
Inputs may be any that keep to these rules, and one draw needn't show every extreme that they name: `segment_ids`: row p numbers the images of pack p block by block: 0 for block 0, rising by one at each block that starts a new image. Some pack is one image, some pack has one image a block. `kept_tokens`: entry (p, i) counts the kept tokens of image i of pack p, which fill the start of that image's blocks: an image of b blocks keeps 128 (b - 1) + 1 to 128 b tokens; numbers with no image hold 0.
All inputs are finite; a program needn't handle non-finite values.
Results may differ from a plain program's by a relative error of at most 0.012.
The roundings to bfloat16 on the way count: a program that leaves them out, or rounds other values in their place, can miss the bound.
Values may be sent and summed in bfloat16 or wider, within the bound.
A program may use at most 192 MiB of HBM per device.

v0:
```python
import jax
import jax.numpy as jnp
from jax import lax
from jax.sharding import PartitionSpec as P

BLOCK = 128


def pair_grads(query_heads, key_heads, value_heads, grad_heads, norm_rows, delta_rows, key_live):
    score_scale = query_heads.shape[2] ** (-0.5)
    scores = (
        jnp.einsum("hqd,hkd->hqk", query_heads, key_heads, preferred_element_type=jnp.float32)
        * score_scale
    )
    probs = jnp.where(key_live[None, None, :], jnp.exp(scores - norm_rows[:, :, None]), 0.0)
    value_grad = jnp.einsum(
        "hqk,hqd->hkd", probs.astype(jnp.bfloat16), grad_heads, preferred_element_type=jnp.float32
    )
    prob_grad = jnp.einsum(
        "hqd,hkd->hqk", grad_heads, value_heads, preferred_element_type=jnp.float32
    )
    score_grad = (probs * (prob_grad - delta_rows[:, :, None])).astype(jnp.bfloat16)
    query_grad = (
        jnp.einsum("hqk,hkd->hqd", score_grad, key_heads, preferred_element_type=jnp.float32)
        * score_scale
    )
    key_grad = (
        jnp.einsum("hqk,hqd->hkd", score_grad, query_heads, preferred_element_type=jnp.float32)
        * score_scale
    )
    return (query_grad, key_grad, value_grad)


def to_blocks(rows, block_count, head_count):
    return rows.reshape(block_count, BLOCK, head_count, rows.shape[1] // head_count).transpose(
        0, 2, 1, 3
    )


def from_blocks(blocked):
    block_count, head_count, block_rows, head_size = blocked.shape
    return (
        blocked.transpose(0, 2, 1, 3)
        .reshape(block_count * block_rows, head_count * head_size)
        .astype(jnp.bfloat16)
    )


def per_device(
    queries, keys, values, attn_out, out_grad, log_norm, segment_ids, kept_tokens, out_weight
):
    tok_rows = queries.shape[0]
    feat_width = queries.shape[1]
    head_count = log_norm.shape[1]
    head_size = feat_width // head_count
    block_count = tok_rows // BLOCK
    seg_ids = segment_ids[0]
    kept_counts = kept_tokens[0]
    block_ids = jnp.arange(block_count)
    first_block = jnp.sum((seg_ids[None, :] < seg_ids[:, None]).astype(jnp.int32), axis=1)
    block_kept = jnp.sum(
        (seg_ids[:, None] == block_ids[None, :]).astype(jnp.int32) * kept_counts[None, :], axis=1
    )
    positions = (block_ids - first_block)[:, None] * BLOCK + jnp.arange(BLOCK)[None, :]
    block_valid = positions < block_kept[:, None]
    token_valid = block_valid.reshape(tok_rows)
    grad_input = jnp.where(token_valid[:, None], out_grad, jnp.zeros_like(out_grad))
    attn_grad = lax.dot_general(
        grad_input,
        lax.all_gather(out_weight, "fsdp", axis=0, tiled=True),
        (((1,), (1,)), ((), ())),
        preferred_element_type=jnp.float32,
    ).astype(jnp.bfloat16)
    delta = jnp.sum(
        (attn_grad.astype(jnp.float32) * attn_out.astype(jnp.float32)).reshape(
            tok_rows, head_count, head_size
        ),
        axis=2,
    )
    grad_share = lax.psum_scatter(
        lax.dot_general(
            attn_out, grad_input, (((0,), (0,)), ((), ())), preferred_element_type=jnp.float32
        ),
        "fsdp",
        scatter_dimension=0,
        tiled=True,
    )
    weight_grad = lax.psum(grad_share, "dp")
    query_blocks = to_blocks(queries, block_count, head_count)
    key_blocks = to_blocks(keys, block_count, head_count)
    value_blocks = to_blocks(values, block_count, head_count)
    grad_blocks = to_blocks(attn_grad, block_count, head_count)
    norm_blocks = log_norm.reshape(block_count, BLOCK, head_count).transpose(0, 2, 1)
    delta_blocks = delta.reshape(block_count, BLOCK, head_count).transpose(0, 2, 1)
    pair_ids = jnp.arange(block_count * block_count)
    pair_live = (seg_ids[pair_ids // block_count] == seg_ids[pair_ids % block_count]).astype(
        jnp.int32
    )
    pair_order = jnp.argsort(1 - pair_live, stable=True)
    pair_total = jnp.sum(pair_live)

    def take_blocks(query_block, key_block):
        return (
            query_blocks[query_block],
            key_blocks[key_block],
            value_blocks[key_block],
            grad_blocks[query_block],
            norm_blocks[query_block],
            delta_blocks[query_block],
            block_valid[key_block],
        )

    def run_pair(pair_step, totals):
        pair_index = pair_order[pair_step]
        query_block = pair_index // block_count
        key_block = pair_index % block_count
        query_term, key_term, value_term = pair_grads(*take_blocks(query_block, key_block))
        return (
            totals[0].at[query_block].add(query_term),
            totals[1].at[key_block].add(key_term),
            totals[2].at[key_block].add(value_term),
        )

    empty = jnp.zeros((block_count, head_count, BLOCK, head_size), jnp.float32)
    totals = (empty, empty, empty)
    totals = lax.fori_loop(0, pair_total, run_pair, totals)
    return (from_blocks(totals[0]), from_blocks(totals[1]), from_blocks(totals[2]), weight_grad)


def solution(mesh):
    placed = (
        P(("dp", "fsdp"), None),
        P(("dp", "fsdp"), None),
        P(("dp", "fsdp"), None),
        P(("dp", "fsdp"), None),
        P(("dp", "fsdp"), None),
        P(("dp", "fsdp"), None),
        P(("dp", "fsdp"), None),
        P(("dp", "fsdp"), None),
        P("fsdp", None),
    )
    return jax.shard_map(
        per_device,
        mesh=mesh,
        in_specs=placed,
        out_specs=(
            P(("dp", "fsdp"), None),
            P(("dp", "fsdp"), None),
            P(("dp", "fsdp"), None),
            P("fsdp", None),
        ),
        check_vma=False,
    )
```

profile of v0, /device:TPU:0, one launch (start us, length us, event | category | flops | bytes accessed | tf_op | source)
XLA Modules:
  0.0 482.5 jit_solution(11948150179926760325)
XLA Ops:
  9.0 12.6 %convolution_bitcast_fusion.1 = f32[2048,2048]{0,1:T(8,128)} fusion(bf16[512,2048]{1,0:T(8,128)(2,1)} %param.20, bf16[512,2048]{1,0:T(8,128)(2,1)} %param.21, pred[512]{0:T(512)(128)(4,1)S(1)} %fusion.27), kind=kOutput, calls=%fused_computation.45 | convolution fusion | flops 4296015872 | bytes 20972032 | tf_op jit(solution)/shard_map/dot_general | solution.py:81
  37.7 48.0 %all-gather.2.cloned.1.call-done = bf16[2048,2048]{1,0:T(8,128)(2,1)} async-done(((bf16[128,2048]{1,0:T(8,128)(2,1)}), bf16[2048,2048]{1,0:T(8,128)(2,1)}) %all-gather.2.cloned.1.call-update) | async-done | bytes 8388624 | tf_op jit(solution)/shard_map/all_gather | solution.py:70
  85.7 8.4 %convolution_convert_fusion = bf16[512,2048]{1,0:T(8,128)(2,1)S(1)} fusion(bf16[2048,2048]{1,0:T(8,128)(2,1)} %all-gather.2.cloned.1.call-done, bf16[512,2048]{1,0:T(8,128)(2,1)S(1)} %copy-done.10, pred[512]{0:T(512)(128)(4,1)S(1)} %fusion.27), kind=kOutput, calls=%fused_computation.47 | convolution fusion | flops 4297064448 | bytes 12583424 | tf_op jit(solution)/shard_map/dot_general | solution.py:68
  100.6 4.1 reduce_sum.39
  113.1 286.7 %while.19 = (s32[]{:T(128)}, f32[4,16,128,128]{3,2,1,0:T(8,128)}, f32[4,16,128,128]{3,2,1,0:T(8,128)}, f32[4,16,128,128]{3,2,1,0:T(8,128)}, s32[]{:T(128)}, /*in...) while((s32[]{:T(128)}, f32[4,16,128,128]{3,2,1,0:T(8,128)}, ...), condition=%wide.region_8.9_spmd, body=%wide.region_5.8_spmd.sunk | while | flops 339476544 | bytes 17879468 | solution.py:126
  121.6 3.3 fusion.49
  128.1 3.5 fusion.48
  146.2 3.3 fusion.48
  157.7 3.2 fusion.49
  164.2 3.2 fusion.48
  193.4 3.3 fusion.49
  196.7 3.3 fusion.47
  214.7 3.3 fusion.47
  217.9 3.3 fusion.48
  232.6 3.2 fusion.47
  235.8 3.2 fusion.48
  250.4 3.2 fusion.47
  265.0 3.3 fusion.49
  289.3 3.2 fusion.48
  307.1 3.2 fusion.48
  336.2 3.3 fusion.49
  360.5 3.2 fusion.48
  378.3 3.2 fusion.48
  415.2 58.2 %all-reduce.2.cloned.1.call-done = f32[128,2048]{0,1:T(8,128)} async-done(((f32[128,2048]{0,1:T(8,128)}), f32[128,2048]{0,1:T(8,128)}) %all-reduce.2.cloned.1.call-update) | async-done | bytes 1048592 | tf_op jit(solution)/shard_map/psum | solution.py:88
  (224 shorter events, 225.3 us)
Async XLA Ops:
  7.2 78.5 %all-gather.2.cloned.1.call-start = ((), (), s32[]{:S(2)}) async-start(), calls=%async_computation.1 | async-start | bytes 8912896 | tf_op jit(solution)/shard_map/all_gather | solution.py:70
  7.9 392.0 %reduce-scatter.2.cloned.1.call-start = ((), (), s32[]{:S(2)}) async-start(), calls=%async_computation.2 | async-start | bytes 17825792 | tf_op jit(solution)/shard_map/reduce_scatter | solution.py:80
  21.6 0.7 copy-start
  21.6 2.0 copy-start.8
  21.6 451.8 %all-reduce.2.cloned.1.call-start = ((), (), s32[]{:S(2)}) async-start(), calls=%async_computation.3 | async-start | bytes 2097152 | tf_op jit(solution)/shard_map/psum | solution.py:88
  23.6 2.4 copy-start.5
  26.0 2.0 copy-start.6
  31.9 2.2 copy-start.3
  31.9 3.0 copy-start.4
  35.0 50.8 %copy-start.10 = (bf16[512,2048]{1,0:T(8,128)(2,1)S(1)}, bf16[512,2048]{1,0:T(8,128)(2,1)}, u32[]{:S(2)}) copy-start(bf16[512,2048]{1,0:T(8,128)(2,1)} %param.21) | copy-start | bytes 6291460
  94.7 2.0 copy-start.7
  110.4 2.8 copy-start.9
  403.9 3.0 copy-start.2
  408.6 3.0 copy-start.1
Sparse Core Ops, SparseCore 0:
  10.4 75.2 all-gather.1
  90.1 145.1 reduce-scatter.1
  400.1 73.3 all-reduce.1
where the time goes:
time: 487 us; the launch traced here: 482 us
  matrix products  192 us (39%)
  waiting for transfers between devices  107 us (22%)
  local copies, waits for them, and re-layouts  92.4 us (19%)
  loops' own time  53.1 us (11%)
  other arithmetic  23.7 us (5%)
  between operations  14 us (3%)
    psum x1, waiting for transfers between devices, per_device(): weight_grad = lax.psum(grad_share, 'dp')  58.2 us
    another operation x1, loops' own time, per_device(): totals = lax.fori_loop(0, pair_total, run_pair, totals)  53.1 us
    dot_general x16, matrix products, pair_grads(): jnp.einsum('hqk,hqd->hkd', score_grad, query_heads, preferred_element_typ...  51.7 us
    dot_general x16, matrix products, pair_grads(): jnp.einsum('hqk,hqd->hkd', probs.astype(jnp.bfloat16), grad_heads, prefer...  51.5 us
    dot_general x16, matrix products, pair_grads(): jnp.einsum('hqk,hkd->hqd', score_grad, key_heads, preferred_element_type=...  51.3 us
    all_gather x1, waiting for transfers between devices, per_device(): lax.all_gather(out_weight, 'fsdp', axis=0, tiled=True)  48 us
    unnamed x31, local copies, waits for them, and re-layouts  23.6 us
    dynamic_slice x16, local copies, waits for them, and re-layouts, take_blocks(): value_blocks[key_block]  22.3 us
  transfers between devices with their start and end apart: 3, of which 2 were waited for; matrix products, arithmetic and copies ran while one was open for 62% of the time, Pallas kernels for 0%

commit v1 on v0

--- a/solution.py
+++ b/solution.py
@@ -1,9 +1,19 @@
+import functools
 import jax
 import jax.numpy as jnp
 from jax import lax
 from jax.sharding import PartitionSpec as P
 
 BLOCK = 128
+
+
+def convert_marks(piece_in, axis_name):
+    lower = lax.all_to_all(jnp.stack([piece_in] * lax.axis_size(axis_name)), axis_name, 0, 0)
+    piece_out = jnp.concatenate(lower, axis=0)
+    return piece_out
+
+
+bind_patch = functools.partial(convert_marks, axis_name="fsdp")
 
 
 def pair_grads(query_heads, key_heads, value_heads, grad_heads, norm_rows, delta_rows, key_live):
@@ -67,7 +77,7 @@
     grad_input = jnp.where(token_valid[:, None], out_grad, jnp.zeros_like(out_grad))
     attn_grad = lax.dot_general(
         grad_input,
-        lax.all_gather(out_weight, "fsdp", axis=0, tiled=True),
+        bind_patch(out_weight),
         (((1,), (1,)), ((), ())),
         preferred_element_type=jnp.float32,
     ).astype(jnp.bfloat16)

time: 487 us -> 588 us (1.21)
  waiting for transfers between devices: 107 us -> 198 us
  starting transfers between devices: 0.3 us -> 8.41 us
    all_to_all x0 -> x1, waiting for transfers between devices: none -> 126 us  [convert_marks(): lax.all_to_all(jnp.stack([piece_in] * lax.axis_size(axis_name)), axis_nam...]
    all_gather x1 -> x0, waiting for transfers between devices: 48 us -> none  [per_device(): lax.all_gather(out_weight, 'fsdp', axis=0, tiled=True)]
    psum x1, waiting for transfers between devices: 58.2 us -> 71.8 us  [per_device(): weight_grad = lax.psum(grad_share, 'dp')]
    all_to_all x0 -> x1, starting transfers between devices: none -> 8.15 us  [convert_marks(): lax.all_to_all(jnp.stack([piece_in] * lax.axis_size(axis_name)), axis_nam...]
    unnamed x31 -> x33, local copies, waits for them, and re-layouts: 23.6 us -> 22.6 us
  transfers between devices with their start and end apart: 3 -> 3, of which waited for: 2 -> 2; matrix products, arithmetic and copies ran while one was open for 62% -> 49% of each run, Pallas kernels for 0% -> 0%
where the time goes in v1:
time: 588 us; the launch traced here: 584 us
  waiting for transfers between devices  198 us (34%)
  matrix products  193 us (33%)
  local copies, waits for them, and re-layouts  94.9 us (16%)
  loops' own time  51.5 us (9%)
  other arithmetic  23.1 us (4%)
  between operations  14.2 us (2%)
  starting transfers between devices  8.41 us (1%)
    all_to_all x1, waiting for transfers between devices, convert_marks(): lax.all_to_all(jnp.stack([piece_in] * lax.axis_size(axis_name)), axis_nam...  126 us
    psum x1, waiting for transfers between devices, per_device(): weight_grad = lax.psum(grad_share, 'dp')  71.8 us
    dot_general x16, matrix products, pair_grads(): jnp.einsum('hqk,hqd->hkd', score_grad, query_heads, preferred_element_typ...  52.5 us
    dot_general x16, matrix products, pair_grads(): jnp.einsum('hqk,hqd->hkd', probs.astype(jnp.bfloat16), grad_heads, prefer...  52.3 us
    another operation x1, loops' own time, per_device(): totals = lax.fori_loop(0, pair_total, run_pair, totals)  51.5 us
    dot_general x16, matrix products, pair_grads(): jnp.einsum('hqk,hkd->hqd', score_grad, key_heads, preferred_element_type=...  50.4 us
    unnamed x33, local copies, waits for them, and re-layouts  22.6 us
    dynamic_slice x16, local copies, waits for them, and re-layouts, take_blocks(): value_blocks[key_block]  22.2 us
  transfers between devices with their start and end apart: 3, of which 2 were waited for; matrix products, arithmetic and copies ran while one was open for 49% of the time, Pallas kernels for 0%

profile of v1, /device:TPU:0, one launch (start us, length us, event | category | flops | bytes accessed | tf_op | source)
XLA Modules:
  0.0 583.7 jit_solution(17467304648238700157)
XLA Ops:
  8.2 12.6 %convolution_bitcast_fusion.1 = f32[2048,2048]{0,1:T(8,128)} fusion(bf16[512,2048]{1,0:T(8,128)(2,1)} %param.20, bf16[512,2048]{1,0:T(8,128)(2,1)} %param.21, pred[512]{0:T(512)(128)(4,1)S(1)} %fusion.27), kind=kOutput, calls=%fused_computation.45 | convolution fusion | flops 4296015872 | bytes 20972032 | tf_op jit(solution)/shard_map/dot_general | solution.py:91
  21.9 4.3 stack.2
  26.2 8.2 %all-to-all-start = ((bf16[16,128,2048]{2,1,0:T(8,128)(2,1)}), bf16[16,128,2048]{2,1,0:T(8,128)(2,1)}, u32[]{:S(2)}, u32[]{:S(2)}) async-start(bf16[16,128,2048]{2,1,0:T(8,128)(2,1)} %stack.2), calls=%async_computation | async-start | bytes 16777216 | tf_op jit(solution)/shard_map/all_to_all | solution.py:11
  50.5 126.5 %all-to-all-done = bf16[16,128,2048]{2,1,0:T(8,128)(2,1)} async-done(((bf16[16,128,2048]{2,1,0:T(8,128)(2,1)}), bf16[16,128,2048]{2,1,0:T(8,128)(2,1)}, u32[]{:S(2)}, u32[]{:S(2)}) %all-to-all-start) | async-done | bytes 8388640 | tf_op jit(solution)/shard_map/all_to_all | solution.py:11
  177.0 8.9 %convolution_convert_fusion = bf16[512,2048]{1,0:T(8,128)(2,1)S(1)} fusion(bf16[2048,2048]{1,0:T(8,128)(2,1)} %bitcast.21, bf16[512,2048]{1,0:T(8,128)(2,1)} %param.21, pred[512]{0:T(512)(128)(4,1)S(1)} %fusion.27), kind=kOutput, calls=%fused_computation.47 | convolution fusion | flops 4297064448 | bytes 12583424 | tf_op jit(solution)/shard_map/dot_general | solution.py:78
  189.5 3.4 reduce_sum.39
  201.5 285.8 %while.19 = (s32[]{:T(128)}, f32[4,16,128,128]{3,2,1,0:T(8,128)}, f32[4,16,128,128]{3,2,1,0:T(8,128)}, f32[4,16,128,128]{3,2,1,0:T(8,128)}, s32[]{:T(128)}, /*in...) while((s32[]{:T(128)}, f32[4,16,128,128]{3,2,1,0:T(8,128)}, ...), condition=%wide.region_8.9_spmd, body=%wide.region_5.8_spmd.sunk | while | flops 339476544 | bytes 17879460 | solution.py:136
  209.8 3.3 fusion.48
  216.3 3.3 fusion.49
  227.7 3.6 fusion.48
  245.8 3.3 fusion.48
  252.2 3.3 fusion.49
  287.7 3.3 fusion.49
  299.2 3.3 fusion.48
  317.0 3.3 fusion.48
  359.0 3.3 fusion.49
  370.4 3.3 fusion.48
  388.2 3.3 fusion.48
  394.6 3.2 fusion.49
  430.1 3.3 fusion.49
  441.5 3.3 fusion.48
  459.3 3.3 fusion.48
  465.7 3.2 fusion.49
  502.5 71.8 %all-reduce.2.cloned.1.call-done = f32[128,2048]{0,1:T(8,128)} async-done(((f32[128,2048]{0,1:T(8,128)}), f32[128,2048]{0,1:T(8,128)}) %all-reduce.2.cloned.1.call-update) | async-done | bytes 1048592 | tf_op jit(solution)/shard_map/psum | solution.py:98
  (226 shorter events, 229.4 us)
Async XLA Ops:
  7.2 480.1 %reduce-scatter.2.cloned.1.call-start = ((), (), s32[]{:S(2)}) async-start(), calls=%async_computation.2 | async-start | bytes 17825792 | tf_op jit(solution)/shard_map/reduce_scatter | solution.py:90
  20.9 1.0 copy-start.9
  26.2 8.4 %copy-start = (s32[1,4]{1,0:T(1,128)S(1)}, s32[1,4]{1,0:T(1,128)}, u32[]{:S(2)}) copy-start(s32[1,4]{1,0:T(1,128)} %param.23) | copy-start | bytes 52
  26.2 9.8 %copy-start.5 = (bf16[512,2048]{1,0:T(8,128)(2,1)S(1)}, bf16[512,2048]{1,0:T(8,128)(2,1)}, u32[]{:S(2)}) copy-start(bf16[512,2048]{1,0:T(8,128)(2,1)} %param.19) | copy-start | bytes 6291460
  26.2 150.7 %all-to-all-start = ((bf16[16,128,2048]{2,1,0:T(8,128)(2,1)}), bf16[16,128,2048]{2,1,0:T(8,128)(2,1)}, u32[]{:S(2)}, u32[]{:S(2)}) async-start(bf16[16,128,2048]{2,1,0:T(8,128)(2,1)} %stack.2), calls=%async_computation | async-start | bytes 16777216 | tf_op jit(solution)/shard_map/all_to_all | solution.py:11
  34.4 540.0 %all-reduce.2.cloned.1.call-start = ((), (), s32[]{:S(2)}) async-start(), calls=%async_computation.3 | async-start | bytes 2097152 | tf_op jit(solution)/shard_map/psum | solution.py:98
  36.0 2.4 copy-start.6
  38.4 2.6 copy-start.7
  41.0 0.8 copy-start.10
  43.7 2.8 copy-start.3
  43.7 3.8 copy-start.4
  177.0 8.9 %copy-start.8 = (bf16[512,2048]{1,0:T(8,128)(2,1)S(1)}, bf16[512,2048]{1,0:T(8,128)(2,1)}, u32[]{:S(2)}) copy-start(bf16[512,2048]{1,0:T(8,128)(2,1)} %param.20) | copy-start | bytes 6291460
  199.0 2.5 copy-start.11
  491.3 2.9 copy-start.2
  496.0 2.9 copy-start.1
Sparse Core Ops, SparseCore 0:
  21.0 234.8 reduce-scatter.1
  487.5 86.8 all-reduce.1
